TPU v7x, 32 devices: a whole 2x2x4 slice. The times are simulated.
32 devices in a mesh: gy: 8 (over y, x, core), gx: 4 (over z).
Axes of the slice: x: 2, y: 2, z: 4, core: 2. Of those that a mesh axis runs over, the one named last changes fastest.
Arguments:
- inputs: bfloat16 [1, 512, 256, 384], P(None, 'gy', 'gx'), may hold values from -6 to 6
- nearby_kernel: bfloat16 [3, 3, 384, 384], replicated, may hold values from -0.109375 to 0.109375
- nearby_bias: float32 [384], replicated, may hold values from -3 to 3
- distant_kernel: bfloat16 [3, 3, 384, 384], replicated, may hold values from -0.109375 to 0.109375
- distant_bias: float32 [384], replicated, may hold values from -3 to 3
Outputs:
- outputs: bfloat16 [1, 512, 256, 384], P(None, 'gy', 'gx')
All inputs are finite; a program needn't handle non-finite values.
Results may differ from a plain program's by a relative error of at most 0.004.
Values may be sent and summed in bfloat16 or wider, within the bound.
A program may use at most 128 MiB of HBM per device.

v0:
```python
import functools

import jax
import jax.numpy as jnp
from jax import lax
from jax.experimental import pallas as pl
from jax.experimental.pallas import tpu as pltpu
from jax.sharding import PartitionSpec as P

MESH = pl.DeviceIdType.MESH
D = 4
DIRS = [(-1, 0), (1, 0), (0, -1), (0, 1), (-1, -1), (-1, 1), (1, -1), (1, 1)]


def gelu(v):
    return v * (1.0 + lax.erf(v * 0.7071067811865476)) * 0.5


def body(ny, nx, x_ref, w1_ref, b1_ref, w2_ref, b2_ref, o_ref,
         xp, w1, w2, h, hl, hr, su, sd, ru, rd, own, ob,
         halo_s, halo_r, loc, hs, hrv, ps, prv, osem):
    gy = lax.axis_index("gy")
    gx = lax.axis_index("gx")
    n, m, c = h.shape
    g = n

    def there(dy, dx):
        ok = None
        for idx, d, size in ((gy, dy, ny), (gx, dx, nx)):
            if d:
                t = idx > 0 if d < 0 else idx < size - 1
                ok = t if ok is None else jnp.logical_and(ok, t)
        return ok

    def dev(dy, dx):
        return (lax.rem(gy + dy + ny, ny), lax.rem(gx + dx + nx, nx))

    load_x = pltpu.make_async_copy(x_ref, xp.at[pl.ds(1, g), pl.ds(1, g)], loc.at[0])
    load_w1 = pltpu.make_async_copy(w1_ref, w1, loc.at[1])
    load_w2 = pltpu.make_async_copy(w2_ref, w2, loc.at[2])
    load_x.start()
    load_w1.start()
    load_w2.start()

    edge = jnp.zeros((g + 2, 16, c), xp.dtype)
    xp[0] = edge
    xp[g + 1] = edge
    xp[pl.ds(1, g), 0] = edge[:g]
    xp[pl.ds(1, g), g + 1] = edge[:g]

    barrier = pltpu.get_barrier_semaphore()
    for d in DIRS:
        @pl.when(there(*d))
        def _(d=d):
            pl.semaphore_signal(barrier, inc=1, device_id=dev(*d), device_id_type=MESH)
    pl.semaphore_wait(barrier, sum(there(*d).astype(jnp.int32) for d in DIRS))

    def halo(i):
        dy, dx = DIRS[i]
        src = [0 if s < 0 else g - 1 if s > 0 else None for s in (dy, dx)]
        src = tuple(pl.ds(0, g) if s is None else pl.ds(s, 1) for s in src)
        dst = [g + 1 if s < 0 else 0 if s > 0 else None for s in (dy, dx)]
        dst = tuple(pl.ds(1, g) if s is None else pl.ds(s, 1) for s in dst)
        return pltpu.make_async_remote_copy(
            src_ref=x_ref.at[src], dst_ref=xp.at[dst], send_sem=halo_s.at[i],
            recv_sem=halo_r.at[i], device_id=dev(dy, dx), device_id_type=MESH)

    for i, d in enumerate(DIRS):
        @pl.when(there(*d))
        def _(i=i):
            halo(i).start()

    for buf, d in ((hl, (0, -1)), (hr, (0, 1)), (ru, (-1, 0)), (rd, (1, 0))):
        @pl.when(jnp.logical_not(there(*d)))
        def _(buf=buf):
            def zero(k, carry):
                buf[k] = jnp.zeros((m, c), buf.dtype)
                return carry
            lax.fori_loop(0, n, zero, 0)

    load_x.wait()
    load_w1.wait()
    for i, d in enumerate(DIRS):
        @pl.when(there(-d[0], -d[1]))
        def _(i=i):
            halo(i).wait_recv()

    def send_h(k, right):
        return pltpu.make_async_remote_copy(
            src_ref=h.at[k], dst_ref=(hl if right else hr).at[k],
            send_sem=hs.at[int(right), k], recv_sem=hrv.at[int(right), k],
            device_id=dev(0, 1 if right else -1), device_id_type=MESH)

    def send_p(k, down):
        return pltpu.make_async_remote_copy(
            src_ref=(sd if down else su).at[k], dst_ref=(ru if down else rd).at[k],
            send_sem=ps.at[int(down), k], recv_sem=prv.at[int(down), k],
            device_id=dev(1 if down else -1, 0), device_id_type=MESH)

    has_l, has_r, has_u, has_d = there(0, -1), there(0, 1), there(-1, 0), there(1, 0)

    def near(k, carry):
        acc = None
        for a in range(3):
            for e in range(3):
                lhs = xp[k + a, pl.ds(e, g)].reshape(m, c)
                t = jnp.dot(lhs, w1[a * 3 + e], preferred_element_type=jnp.float32)
                acc = t if acc is None else acc + t
        h[k] = gelu(acc + b1_ref[...]).astype(h.dtype)

        @pl.when(has_r)
        def _():
            send_h(k, True).start()

        @pl.when(has_l)
        def _():
            send_h(k, False).start()
        return carry

    lax.fori_loop(0, n, near, 0)
    load_w2.wait()

    def finish(k):
        @pl.when(has_u)
        def _():
            send_p(k, True).wait_recv()

        @pl.when(has_d)
        def _():
            send_p(k, False).wait_recv()
        v = own[k] + ru[k].astype(jnp.float32) + rd[k].astype(jnp.float32) + b2_ref[...]
        branch = gelu(v).astype(jnp.bfloat16).astype(jnp.float32)
        x = xp[k + 1, pl.ds(1, g)].reshape(m, c).astype(jnp.float32)
        ob[k] = (x + branch).astype(ob.dtype)
        pltpu.make_async_copy(ob.at[k], o_ref.at[k], osem.at[k]).start()

    def far_sum(k, a):
        acc = None
        for e, v in enumerate((hl, h, hr)):
            t = jnp.dot(v[k], w2[a * 3 + e], preferred_element_type=jnp.float32)
            acc = t if acc is None else acc + t
        return acc

    def far(k, carry):
        @pl.when(has_l)
        def _():
            send_h(k, True).wait_recv()

        @pl.when(has_r)
        def _():
            send_h(k, False).wait_recv()
        sd[k] = far_sum(k, 0).astype(sd.dtype)
        su[k] = far_sum(k, 2).astype(su.dtype)

        @pl.when(has_d)
        def _():
            send_p(k, True).start()

        @pl.when(has_u)
        def _():
            send_p(k, False).start()
        own[k] = far_sum(k, 1)

        @pl.when(k > 0)
        def _():
            finish(k - 1)
        return carry

    lax.fori_loop(0, n, far, 0)
    finish(n - 1)

    for i, d in enumerate(DIRS):
        @pl.when(there(*d))
        def _(i=i):
            halo(i).wait_send()

    def drain(k, carry):
        for ok, make, flag in ((has_r, send_h, True), (has_l, send_h, False),
                               (has_d, send_p, True), (has_u, send_p, False)):
            @pl.when(ok)
            def _(make=make, flag=flag):
                make(k, flag).wait_send()
        pltpu.make_async_copy(ob.at[k], o_ref.at[k], osem.at[k]).wait()
        return carry

    lax.fori_loop(0, n, drain, 0)


def on_device(inputs, nearby_kernel, nearby_bias, distant_kernel, distant_bias):
    _, rows, cols, c = inputs.shape
    ny, nx = lax.axis_size("gy"), lax.axis_size("gx")
    g = rows // D
    m = cols * D
    blocks = inputs.reshape(g, D, cols // D, D, c).transpose(0, 2, 1, 3, 4).reshape(g, g, D * D, c)
    bf, f32 = jnp.bfloat16, jnp.float32
    tile = pltpu.VMEM((g, m, c), bf)
    dma = pltpu.SemaphoreType.DMA
    hbm = pl.BlockSpec(memory_space=pl.ANY)
    vmem = pl.BlockSpec(memory_space=pltpu.VMEM)
    out = pl.pallas_call(
        functools.partial(body, ny, nx),
        out_shape=jax.ShapeDtypeStruct((g, m, c), bf),
        in_specs=[hbm, hbm, vmem, hbm, vmem],
        out_specs=hbm,
        scratch_shapes=[
            pltpu.VMEM((g + 2, g + 2, D * D, c), bf),
            pltpu.VMEM((9, c, c), bf),
            pltpu.VMEM((9, c, c), bf),
            tile, tile, tile, tile, tile, tile, tile,
            pltpu.VMEM((g, m, c), f32),
            tile,
            dma((8,)), dma((8,)), dma((3,)),
            dma((2, g)), dma((2, g)), dma((2, g)), dma((2, g)), dma((g,)),
        ],
        compiler_params=pltpu.CompilerParams(
            collective_id=0, has_side_effects=True, vmem_limit_bytes=56 * 1024 * 1024),
        cost_estimate=pl.CostEstimate(
            flops=36 * rows * cols * c * c, bytes_accessed=16 * 2**20, transcendentals=0),
    )(blocks, nearby_kernel.reshape(9, c, c), nearby_bias.reshape(1, c),
      distant_kernel.reshape(9, c, c), distant_bias.reshape(1, c))
    return out.reshape(g, g, D, D, c).transpose(0, 2, 1, 3, 4).reshape(1, rows, cols, c)


def solution(mesh):
    placed = (P(None, "gy", "gx", None), P(), P(), P(), P())
    return jax.shard_map(
        on_device, mesh=mesh, in_specs=placed, out_specs=P(None, "gy", "gx", None), check_vma=False
    )
```

profile of v0, /device:TPU:1, one launch (start us, length us, event | category | flops | bytes accessed | tf_op | source)
XLA Modules:
  0.0 133.7 jit_solution(9253312238104989160)
XLA Ops:
  0.0 1.3 reshape.27.b1_ref
  1.3 1.2 reshape.29.b2_ref
  2.5 6.2 %reshape.24 = bf16[16,4,16,4,384]{4,3,2,1,0:T(4,128)(2,1)} reshape(bf16[1,64,64,384]{3,2,1,0:T(8,128)(2,1)} %param.5) | data formatting | bytes 6291456 | tf_op jit(solution)/shard_map/reshape | solution.py:194
  8.6 3.1 %copy.9 = bf16[16,4,16,4,384]{4,3,1,2,0:T(4,128)(2,1)S(1)} copy(bf16[16,4,16,4,384]{4,3,2,1,0:T(4,128)(2,1)} %reshape.24) | data formatting | bytes 6291456 | tf_op jit(solution)/shard_map/reshape | solution.py:194
  11.7 2.4 %reshape.25.x_ref = bf16[16,16,16,384]{3,2,1,0:T(8,128)(2,1)} reshape(bf16[16,16,4,4,384]{4,3,2,1,0:T(4,128)(2,1)S(1)} %bitcast.8) | data formatting | bytes 6291456 | tf_op jit(solution)/shard_map/reshape | solution.py:194
  14.1 105.5 %shard_map.55 = bf16[16,256,384]{2,1,0:T(8,128)(2,1)} custom-call(bf16[16,16,16,384]{3,2,1,0:T(8,128)(2,1)} %reshape.25.x_ref, bf16[9,384,384]{2,1,0:T(8,128)(2,1)} %bitcast.10, f32[1,384]{1,0:T(1,128)} %reshape.27.b1_ref, bf16[9,384,384]{2,1,0:T(8,128)(2,1)} %bitcast.11, f32[1,384]{1,0:T(1,128)} %reshape.29.b2_ref), custom_call_target="tpu_custom_call" | custom-call | flops 21743271936 | bytes 16777216 | tf_op jit(solution)/shard_map/pallas_call | solution.py:200
  119.6 4.8 %reshape.30 = bf16[16,16,4,4,384]{4,3,2,1,0:T(4,128)(2,1)S(1)} reshape(bf16[16,256,384]{2,1,0:T(8,128)(2,1)} %shard_map.55) | data formatting | bytes 6291456 | tf_op jit(solution)/shard_map/reshape | solution.py:221
  124.4 3.3 %copy.7 = bf16[16,4,16,4,384]{4,3,2,1,0:T(4,128)(2,1)} copy(bf16[16,4,16,4,384]{4,3,1,2,0:T(4,128)(2,1)S(1)} %bitcast.9) | data formatting | bytes 6291456 | tf_op jit(solution)/shard_map/transpose | solution.py:221
  127.7 5.9 %reshape.31 = bf16[1,64,64,384]{3,2,1,0:T(8,128)(2,1)} reshape(bf16[16,4,16,4,384]{4,3,2,1,0:T(4,128)(2,1)} %copy.7) | data formatting | bytes 6291456 | tf_op jit(solution)/shard_map/reshape | solution.py:221
where the time goes:
time: 134 us
  Pallas kernels  105 us (78%)
  local copies, waits for them, and re-layouts  28.2 us (21%)
    pallas_call x1, Pallas kernels, on_device(): pl.pallas_call(functools.partial(body, ny, nx), out_shape=jax.ShapeDtypeS...  105 us
    reshape x3, local copies, waits for them, and re-layouts, on_device(): inputs.reshape(g, D, cols // D, D, c).transpose(0, 2, 1, 3, 4)  11.6 us
    reshape x2, local copies, waits for them, and re-layouts, on_device(): out.reshape(g, g, D, D, c).transpose(0, 2, 1, 3, 4)  10.8 us
    transpose x1, local copies, waits for them, and re-layouts, on_device(): out.reshape(g, g, D, D, c).transpose(0, 2, 1, 3, 4)  3.32 us

commit v1 on v0

--- a/solution.py
+++ b/solution.py
@@ -9,7 +9,35 @@
 
 MESH = pl.DeviceIdType.MESH
 D = 4
+LAG = 4
+LATE = 2
 DIRS = [(-1, 0), (1, 0), (0, -1), (0, 1), (-1, -1), (-1, 1), (1, -1), (1, 1)]
+
+
+def swap(a, b):
+    n, c = a.size // (8 * a.shape[-1]), a.shape[-1]
+    low = lax.broadcasted_iota(jnp.int32, (n, 8, c), 1) < 4
+    p, q = a.reshape(n, 8, c), b.reshape(n, 8, c)
+    first = jnp.where(low, p, pltpu.roll(q, 4, 1))
+    second = jnp.where(low, pltpu.roll(p, 4, 1), q)
+    return first.reshape(a.shape), second.reshape(a.shape)
+
+
+def to_blocks(v):
+    c = v.shape[-1]
+    t = v.shape[1] // 16
+    v = v.reshape(2, 2, t, 2, 8, c)
+    parts = [swap(v[i, 0], v[i, 1]) for i in range(2)]
+    out = jnp.stack([jnp.stack([parts[i][hi] for i in range(2)], axis=2) for hi in range(2)], axis=2)
+    return out.reshape(4 * t, 16, c)
+
+
+def from_blocks(v):
+    c = v.shape[-1]
+    t = v.shape[0] // 4
+    v = v.reshape(t, 2, 2, 2, 8, c)
+    parts = [swap(v[:, :, 0, i], v[:, :, 1, i]) for i in range(2)]
+    return jnp.stack([parts[i][odd] for i in range(2) for odd in range(2)], axis=0).reshape(4, 16 * t, c)
 
 
 def gelu(v):
@@ -17,7 +45,7 @@
 
 
 def body(ny, nx, x_ref, w1_ref, b1_ref, w2_ref, b2_ref, o_ref,
-         xp, w1, w2, h, hl, hr, su, sd, ru, rd, own, ob,
+         xin, xp, w1, w2, h, hl, hr, su, sd, ru, rd, own, ob,
          halo_s, halo_r, loc, hs, hrv, ps, prv, osem):
     gy = lax.axis_index("gy")
     gx = lax.axis_index("gx")
@@ -35,7 +63,7 @@
     def dev(dy, dx):
         return (lax.rem(gy + dy + ny, ny), lax.rem(gx + dx + nx, nx))
 
-    load_x = pltpu.make_async_copy(x_ref, xp.at[pl.ds(1, g), pl.ds(1, g)], loc.at[0])
+    load_x = pltpu.make_async_copy(x_ref, xin, loc.at[0])
     load_w1 = pltpu.make_async_copy(w1_ref, w1, loc.at[1])
     load_w2 = pltpu.make_async_copy(w2_ref, w2, loc.at[2])
     load_x.start()
@@ -53,16 +81,23 @@
         @pl.when(there(*d))
         def _(d=d):
             pl.semaphore_signal(barrier, inc=1, device_id=dev(*d), device_id_type=MESH)
+    load_x.wait()
+
+    def reorder(k, carry):
+        xp[k + 1, pl.ds(1, g)] = to_blocks(xin[pl.ds(D * k, D)].astype(jnp.float32)).astype(xp.dtype)
+        return carry
+
+    lax.fori_loop(0, g, reorder, 0)
     pl.semaphore_wait(barrier, sum(there(*d).astype(jnp.int32) for d in DIRS))
 
     def halo(i):
         dy, dx = DIRS[i]
-        src = [0 if s < 0 else g - 1 if s > 0 else None for s in (dy, dx)]
-        src = tuple(pl.ds(0, g) if s is None else pl.ds(s, 1) for s in src)
+        src = [1 if s < 0 else g if s > 0 else None for s in (dy, dx)]
+        src = tuple(pl.ds(1, g) if s is None else pl.ds(s, 1) for s in src)
         dst = [g + 1 if s < 0 else 0 if s > 0 else None for s in (dy, dx)]
         dst = tuple(pl.ds(1, g) if s is None else pl.ds(s, 1) for s in dst)
         return pltpu.make_async_remote_copy(
-            src_ref=x_ref.at[src], dst_ref=xp.at[dst], send_sem=halo_s.at[i],
+            src_ref=xp.at[src], dst_ref=xp.at[dst], send_sem=halo_s.at[i],
             recv_sem=halo_r.at[i], device_id=dev(dy, dx), device_id_type=MESH)
 
     for i, d in enumerate(DIRS):
@@ -78,7 +113,6 @@
                 return carry
             lax.fori_loop(0, n, zero, 0)
 
-    load_x.wait()
     load_w1.wait()
     for i, d in enumerate(DIRS):
         @pl.when(there(-d[0], -d[1]))
@@ -99,14 +133,14 @@
 
     has_l, has_r, has_u, has_d = there(0, -1), there(0, 1), there(-1, 0), there(1, 0)
 
-    def near(k, carry):
+    def near(k):
         acc = None
         for a in range(3):
             for e in range(3):
                 lhs = xp[k + a, pl.ds(e, g)].reshape(m, c)
                 t = jnp.dot(lhs, w1[a * 3 + e], preferred_element_type=jnp.float32)
                 acc = t if acc is None else acc + t
-        h[k] = gelu(acc + b1_ref[...]).astype(h.dtype)
+        h[k] = gelu(acc + b1_ref[...].reshape(1, c)).astype(h.dtype)
 
         @pl.when(has_r)
         def _():
@@ -115,10 +149,10 @@
         @pl.when(has_l)
         def _():
             send_h(k, False).start()
-        return carry
-
-    lax.fori_loop(0, n, near, 0)
-    load_w2.wait()
+
+    def store(k):
+        rows = pl.ds(D * k, D)
+        return pltpu.make_async_copy(ob.at[rows], o_ref.at[rows], osem.at[k])
 
     def finish(k):
         @pl.when(has_u)
@@ -128,11 +162,11 @@
         @pl.when(has_d)
         def _():
             send_p(k, False).wait_recv()
-        v = own[k] + ru[k].astype(jnp.float32) + rd[k].astype(jnp.float32) + b2_ref[...]
+        v = own[k] + ru[k].astype(jnp.float32) + rd[k].astype(jnp.float32) + b2_ref[...].reshape(1, c)
         branch = gelu(v).astype(jnp.bfloat16).astype(jnp.float32)
         x = xp[k + 1, pl.ds(1, g)].reshape(m, c).astype(jnp.float32)
-        ob[k] = (x + branch).astype(ob.dtype)
-        pltpu.make_async_copy(ob.at[k], o_ref.at[k], osem.at[k]).start()
+        ob[pl.ds(D * k, D)] = from_blocks((x + branch).reshape(g, 16, c)).astype(ob.dtype)
+        store(k).start()
 
     def far_sum(k, a):
         acc = None
@@ -141,7 +175,7 @@
             acc = t if acc is None else acc + t
         return acc
 
-    def far(k, carry):
+    def far(k):
         @pl.when(has_l)
         def _():
             send_h(k, True).wait_recv()
@@ -161,13 +195,33 @@
             send_p(k, False).start()
         own[k] = far_sum(k, 1)
 
-        @pl.when(k > 0)
-        def _():
-            finish(k - 1)
-        return carry
-
-    lax.fori_loop(0, n, far, 0)
-    finish(n - 1)
+    def ahead(k, carry):
+        near(k)
+        return carry
+
+    def both(k, carry):
+        near(k + LAG)
+        far(k)
+
+        @pl.when(k >= LATE)
+        def _():
+            finish(k - LATE)
+        return carry
+
+    def behind(k, carry):
+        far(k)
+        finish(k - LATE)
+        return carry
+
+    def last(k, carry):
+        finish(k)
+        return carry
+
+    lax.fori_loop(0, LAG, ahead, 0)
+    load_w2.wait()
+    lax.fori_loop(0, n - LAG, both, 0)
+    lax.fori_loop(n - LAG, n, behind, 0)
+    lax.fori_loop(n - LATE, n, last, 0)
 
     for i, d in enumerate(DIRS):
         @pl.when(there(*d))
@@ -180,7 +234,7 @@
             @pl.when(ok)
             def _(make=make, flag=flag):
                 make(k, flag).wait_send()
-        pltpu.make_async_copy(ob.at[k], o_ref.at[k], osem.at[k]).wait()
+        store(k).wait()
         return carry
 
     lax.fori_loop(0, n, drain, 0)
@@ -191,7 +245,6 @@
     ny, nx = lax.axis_size("gy"), lax.axis_size("gx")
     g = rows // D
     m = cols * D
-    blocks = inputs.reshape(g, D, cols // D, D, c).transpose(0, 2, 1, 3, 4).reshape(g, g, D * D, c)
     bf, f32 = jnp.bfloat16, jnp.float32
     tile = pltpu.VMEM((g, m, c), bf)
     dma = pltpu.SemaphoreType.DMA
@@ -199,16 +252,17 @@
     vmem = pl.BlockSpec(memory_space=pltpu.VMEM)
     out = pl.pallas_call(
         functools.partial(body, ny, nx),
-        out_shape=jax.ShapeDtypeStruct((g, m, c), bf),
+        out_shape=jax.ShapeDtypeStruct((rows, cols, c), bf),
         in_specs=[hbm, hbm, vmem, hbm, vmem],
         out_specs=hbm,
         scratch_shapes=[
+            pltpu.VMEM((rows, cols, c), bf),
             pltpu.VMEM((g + 2, g + 2, D * D, c), bf),
             pltpu.VMEM((9, c, c), bf),
             pltpu.VMEM((9, c, c), bf),
             tile, tile, tile, tile, tile, tile, tile,
             pltpu.VMEM((g, m, c), f32),
-            tile,
+            pltpu.VMEM((rows, cols, c), bf),
             dma((8,)), dma((8,)), dma((3,)),
             dma((2, g)), dma((2, g)), dma((2, g)), dma((2, g)), dma((g,)),
         ],
@@ -216,9 +270,9 @@
             collective_id=0, has_side_effects=True, vmem_limit_bytes=56 * 1024 * 1024),
         cost_estimate=pl.CostEstimate(
             flops=36 * rows * cols * c * c, bytes_accessed=16 * 2**20, transcendentals=0),
-    )(blocks, nearby_kernel.reshape(9, c, c), nearby_bias.reshape(1, c),
-      distant_kernel.reshape(9, c, c), distant_bias.reshape(1, c))
-    return out.reshape(g, g, D, D, c).transpose(0, 2, 1, 3, 4).reshape(1, rows, cols, c)
+    )(inputs.reshape(rows, cols, c), nearby_kernel.reshape(9, c, c), nearby_bias,
+      distant_kernel.reshape(9, c, c), distant_bias)
+    return out.reshape(1, rows, cols, c)
 
 
 def solution(mesh):

time: 134 us -> 97.2 us (0.73)
  local copies, waits for them, and re-layouts: 28.2 us -> 3.88 us
  Pallas kernels: 105 us -> 93.2 us
    reshape x7 -> x0, local copies, waits for them, and re-layouts: 24.9 us -> none  [the longest x3 11.6 us: on_device(): inputs.reshape(g, D, cols // D, D, c).transpose(0, 2, 1, 3, 4)]
    pallas_call x1, Pallas kernels: 105 us -> 93.2 us  [on_device(): pl.pallas_call(functools.partial(body, ny, nx), out_shape=jax.ShapeDtypeS...]
    unnamed x0 -> x1, local copies, waits for them, and re-layouts: none -> 3.88 us
    transpose x1 -> x0, local copies, waits for them, and re-layouts: 3.32 us -> none  [on_device(): out.reshape(g, g, D, D, c).transpose(0, 2, 1, 3, 4)]
where the time goes in v1:
time: 97.2 us; the launch traced here: 97 us
  Pallas kernels  93.2 us (96%)
  local copies, waits for them, and re-layouts  3.88 us (4%)
    pallas_call x1, Pallas kernels, on_device(): pl.pallas_call(functools.partial(body, ny, nx), out_shape=jax.ShapeDtypeS...  93.2 us
    unnamed x1, local copies, waits for them, and re-layouts  3.88 us

profile of v1, /device:TPU:1, one launch (start us, length us, event | category | flops | bytes accessed | tf_op | source)
XLA Modules:
  0.0 97.0 jit_solution(17243833787825087247)
XLA Ops:
  0.0 93.2 %shard_map.55 = bf16[64,64,384]{2,1,0:T(8,128)(2,1)} custom-call(bf16[64,64,384]{2,1,0:T(8,128)(2,1)} %bitcast.5, bf16[9,384,384]{2,1,0:T(8,128)(2,1)} %bitcast.6, f32[384]{0:T(512)} %b1_ref.1, bf16[9,384,384]{2,1,0:T(8,128)(2,1)} %bitcast.7, f32[384]{0:T(512)} %b2_ref.1), custom_call_target="tpu_custom_call" | custom-call | flops 21743271936 | bytes 16777216 | tf_op jit(solution)/shard_map/pallas_call | solution.py:253
  93.2 3.9 %copy.7 = bf16[1,64,64,384]{3,2,1,0:T(8,128)(2,1)} copy(bf16[1,64,64,384]{3,2,1,0:T(8,128)(2,1)} %bitcast.4) | data formatting | bytes 6291456

commit v2 on v1

--- a/solution.py
+++ b/solution.py
@@ -9,8 +9,8 @@
 
 MESH = pl.DeviceIdType.MESH
 D = 4
-LAG = 4
-LATE = 2
+LAG = 3
+LATE = 1
 DIRS = [(-1, 0), (1, 0), (0, -1), (0, 1), (-1, -1), (-1, 1), (1, -1), (1, 1)]
 
 
@@ -184,11 +184,11 @@
         def _():
             send_h(k, False).wait_recv()
         sd[k] = far_sum(k, 0).astype(sd.dtype)
+
+        @pl.when(has_d)
+        def _():
+            send_p(k, True).start()
         su[k] = far_sum(k, 2).astype(su.dtype)
-
-        @pl.when(has_d)
-        def _():
-            send_p(k, True).start()
 
         @pl.when(has_u)
         def _():

time: 97.2 us -> 97 us (level)
  no operation moved by 1% of the time
where the time goes in v2:
time: 97 us; the launch traced here: 96.8 us
  Pallas kernels  92.9 us (96%)
  local copies, waits for them, and re-layouts  3.88 us (4%)
    pallas_call x1, Pallas kernels, on_device(): pl.pallas_call(functools.partial(body, ny, nx), out_shape=jax.ShapeDtypeS...  92.9 us
    unnamed x1, local copies, waits for them, and re-layouts  3.88 us

profile of v2, /device:TPU:1, one launch (start us, length us, event | category | flops | bytes accessed | tf_op | source)
XLA Modules:
  0.0 96.8 jit_solution(11769849315483446125)
XLA Ops:
  0.0 92.9 %shard_map.55 = bf16[64,64,384]{2,1,0:T(8,128)(2,1)} custom-call(bf16[64,64,384]{2,1,0:T(8,128)(2,1)} %bitcast.5, bf16[9,384,384]{2,1,0:T(8,128)(2,1)} %bitcast.6, f32[384]{0:T(512)} %b1_ref.1, bf16[9,384,384]{2,1,0:T(8,128)(2,1)} %bitcast.7, f32[384]{0:T(512)} %b2_ref.1), custom_call_target="tpu_custom_call" | custom-call | flops 21743271936 | bytes 16777216 | tf_op jit(solution)/shard_map/pallas_call | solution.py:253
  92.9 3.9 %copy.7 = bf16[1,64,64,384]{3,2,1,0:T(8,128)(2,1)} copy(bf16[1,64,64,384]{3,2,1,0:T(8,128)(2,1)} %bitcast.4) | data formatting | bytes 6291456
